TPU v7x, 512 devices: a whole 4x4x16 slice. The times are simulated.
512 devices in a mesh: dp: 64 (over z, x), sub: 8 (over y, core).
Axes of the slice: x: 4, y: 4, z: 16, core: 2. Of those that a mesh axis runs over, the one named last changes fastest.
Arguments:
- points: bfloat16 [262144, 256], P(('dp', 'sub'))
- candidates: int32 [4, 768], replicated, may hold values from 0 to 262143, as said below
- owner_slot: int32 [3072], replicated, may hold values from 0 to 3071, each once
Outputs:
- centroids: float32 [3072, 256], P(('dp', 'sub'))
- masses: float32 [3072], P(('dp', 'sub'))
- min_dist: float32 [262144], P(('dp', 'sub'))
Inputs may be any that keep to these rules, and one draw needn't show every extreme that they name: In each round the candidates are distinct rows; no device's block of 512 rows holds more than 8 candidates of one round, and in each round some device's block holds exactly 8.
All inputs are finite; a program needn't handle non-finite values.
Results may differ from a plain program's by a relative error of at most 0.00055.
Values may be sent and summed in bfloat16 or wider, within the bound.
A program may use at most 64 MiB of HBM per device.

v0:
```python
import jax
import jax.numpy as jnp
from jax import lax
from jax.sharding import PartitionSpec as P


def pick_rows(round_rows, points, my_device):
    row_count = points.shape[0]
    flat_rows = round_rows.reshape(-1)
    owner_dev = flat_rows // row_count
    local_row = flat_rows % row_count
    mine = owner_dev == my_device
    picked = jnp.where(
        mine[:, None], points[local_row].astype(jnp.float32), jnp.zeros((), jnp.float32)
    )
    return lax.psum(picked, ("dp", "sub")).astype(jnp.bfloat16)


def on_device(points, candidates, owner_slot):
    row_count = points.shape[0]
    width_dim = points.shape[1]
    round_count = candidates.shape[0]
    my_device = lax.axis_index(("dp", "sub"))
    block_rows = min(512, row_count)
    point_norm = jnp.sum(points.astype(jnp.float32) ** 2, axis=1)
    chosen_list = [
        pick_rows(candidates[which_round : which_round + 1], points, my_device)
        for which_round in range(round_count)
    ]
    nearest_parts = [jnp.full((block_rows,), 3e38, jnp.float32)]
    sums_parts = []
    mass_parts = []
    for which_round in range(round_count):
        chosen = chosen_list[which_round]
        cand_norm = jnp.sum(chosen.astype(jnp.float32) ** 2, axis=1)
        dots = lax.dot_general(
            points, chosen, (((1,), (1,)), ((), ())), preferred_element_type=jnp.float32
        )
        dist = point_norm[:, None] + cand_norm[None, :] - 2.0 * dots
        nearest_parts[0] = jnp.minimum(nearest_parts[0], jnp.min(dist, axis=1))
        kernel = jnp.exp(-dist / 0.25).astype(jnp.bfloat16)
        sums_round = lax.dot_general(
            kernel, points, (((0,), (0,)), ((), ())), preferred_element_type=jnp.float32
        )
        mass_round = jnp.sum(kernel.astype(jnp.float32), axis=0)
        sums_parts.append(sums_round)
        mass_parts.append(mass_round)
    partial_sums = jnp.concatenate(sums_parts, axis=0)
    partial_mass = jnp.concatenate(mass_parts, axis=0)
    total_rows = partial_sums.shape[0]
    placed_sums = jnp.zeros((total_rows, width_dim), jnp.float32).at[owner_slot].set(partial_sums)
    placed_mass = jnp.zeros((total_rows,), jnp.float32).at[owner_slot].set(partial_mass)
    summed, masses = (
        lax.psum_scatter(placed_sums, ("dp", "sub"), scatter_dimension=0, tiled=True),
        lax.psum_scatter(placed_mass, ("dp", "sub"), scatter_dimension=0, tiled=True),
    )
    centroids = summed / masses[:, None]
    min_dist = nearest_parts[0]
    return (centroids, masses, min_dist)


def solution(mesh):
    placed = (P(("dp", "sub"), None), P(), P())
    return jax.shard_map(
        on_device,
        mesh=mesh,
        in_specs=placed,
        out_specs=(P(("dp", "sub"), None), P(("dp", "sub")), P(("dp", "sub"))),
        check_vma=False,
    )
```

profile of v0, /device:TPU:6, one launch (start us, length us, event | category | flops | bytes accessed | tf_op | source)
XLA Modules:
  0.0 728.3 jit_solution(3182562303138796579)
XLA Ops:
  7.2 0.0 copy-start
  7.2 0.0 all-reduce.6.cloned.1.call-start
  7.2 0.9 slice_reduce_fusion.3
  8.1 0.9 fusion.31
  9.1 1.1 multiply_reduce_fusion.4
  10.2 0.7 compare_select_fusion
  10.9 0.0 copy-done
  10.9 2.7 gather_fusion.3
  13.6 2.7 gather_fusion.1
  16.3 0.2 convert_select_fusion.2
  16.5 0.2 convert_select_fusion
  16.6 2.7 gather_fusion.2
  19.3 0.2 convert_select_fusion.1
  19.5 3.3 gather_fusion
  22.8 1.2 convert_select_fusion.3
  23.9 187.4 %all-reduce.7 = (bf16[768,256]{1,0:T(8,128)(2,1)}, bf16[768,256]{1,0:T(8,128)(2,1)}, bf16[768,256]{1,0:T(8,128)(2,1)}, bf16[768,256]{1,0:T(8,128)(2,1)}) all-reduce(f32[768,256]{1,0:T(8,128)S(1)} %convert_select_fusion, f32[768,256]{1,0:T(8,128)S(1)} %convert_select_fusion.1, ...), channel_id=1, replica_groups=mesh['dp'=64,'sub'=8] {'dp','sub'}, use_global_device_ids=true, to_apply=%region_7.8 | all-reduce | flops 786432 | bytes 4718592 | tf_op jit(solution)/shard_map/psum | solution.py:16
  211.4 0.0 copy-start.4
  211.4 1.2 multiply_reduce_fusion
  212.6 1.2 multiply_reduce_fusion.1
  213.8 1.2 multiply_reduce_fusion.2
  214.9 1.2 multiply_reduce_fusion.3
  216.1 0.0 copy-done.4
  216.1 0.7 fusion.43
  216.8 0.0 copy-start.3
  216.8 0.4 fusion.13
  217.2 0.6 copy-done.3
  217.8 0.7 fusion.44
  218.5 0.0 copy-start.2
  218.5 0.4 fusion.14
  218.9 0.6 copy-done.2
  219.5 0.7 fusion.45
  220.2 0.0 copy-start.1
  220.2 0.4 fusion.15
  220.6 0.6 copy-done.1
  221.2 0.7 fusion.46
  221.9 0.4 fusion.16
  222.3 17.2 %scatter_custom_fusion = f32[3072,256]{1,0:T(8,128)} fusion(s32[3072]{0:T(1024)S(1)} %compare_select_fusion, f32[768,256]{1,0:T(8,128)S(1)} %fusion.16, f32[]{:T(128)} %constant.110, f32[768,256]{1,0:T(8,128)S(1)} %fusion.15, f32[768,256]{1,0:T(8,128)S(1)} %fusion.14, f32[768,256]{1,0:T(8,128)S(1)} %fusion.13, f32[]{:T(128)} %constant.80.clone.1), kind=kCustom, calls=%fused_computation.6 | custom fusion | flops 2359296 | bytes 6291464 | tf_op jit(solution)/shard_map/scatter | solution.py:51
  239.4 0.0 all-reduce.6.cloned.1.call-update
  239.5 11.8 %scatter_custom_fusion.1 = f32[3072]{0:T(1024)S(1)} fusion(s32[3072]{0:T(1024)S(1)} %compare_select_fusion, f32[3072]{0:T(1024)S(1)} %pad_maximum_fusion, f32[]{:T(128)} %constant.80.clone.1), kind=kCustom, calls=%fused_computation.63 | custom fusion | bytes 12292 | tf_op jit(solution)/shard_map/scatter | solution.py:52
  251.3 101.4 %all-reduce.1 = f32[3072]{0:T(1024)S(1)} all-reduce(f32[3072]{0:T(1024)S(1)} %scatter_custom_fusion.1), channel_id=3, replica_groups=mesh['dp'=64,'sub'=8] {'dp','sub'}, use_global_device_ids=true, to_apply=%region_16.17.clone | all-reduce | flops 3072 | bytes 24576
  352.7 0.1 dynamic-slice.1
  352.8 0.0 copy-start.5
  352.8 0.6 minimum_minimum_fusion
  353.4 366.7 %all-reduce.6.cloned.1.call-done = f32[3072,256]{1,0:T(8,128)} async-done(((f32[3072,256]{1,0:T(8,128)}), f32[3072,256]{1,0:T(8,128)}) %all-reduce.6.cloned.1.call-update) | async-done | bytes 3145744
  720.1 1.4 dynamic-slice_divide_fusion
  721.5 0.0 copy-done.5
  (5 shorter events, 0.0 us)
Async XLA Ops:
  7.2 3.7 copy-start
  7.2 712.9 %all-reduce.6.cloned.1.call-start = ((), (), s32[]{:S(2)}) async-start(), calls=%async_computation | async-start | bytes 6291456
  211.4 4.8 copy-start.4
  216.8 1.0 copy-start.3
  218.5 1.0 copy-start.2
  220.2 1.0 copy-start.1
  352.8 368.7 %copy-start.5 = (f32[6]{0:T(128)}, f32[6]{0:T(128)S(1)}, u32[]{:S(2)}) copy-start(f32[6]{0:T(128)S(1)} %dynamic-slice.1) | copy-start | bytes 76
Sparse Core Ops, SparseCore 0:
  239.6 480.4 all-reduce.5
where the time goes:
time: 729 us; the launch traced here: 728 us
  waiting for transfers between devices  367 us (50%)
  blocking collectives  289 us (40%)
  other arithmetic  28.4 us (4%)
  local copies, waits for them, and re-layouts  25.9 us (4%)
  between operations  14.3 us (2%)
    unnamed x2, waiting for transfers between devices  367 us
    psum x1, blocking collectives, pick_rows(): return lax.psum(picked, ('dp', 'sub')).astype(jnp.bfloat16)  187 us
    unnamed x1, blocking collectives  101 us
    scatter x1, other arithmetic, on_device(): jnp.zeros((total_rows, width_dim), jnp.float32).at[owner_slot]  17.2 us
  transfers between devices with their start and end apart: 1, of which 1 were waited for; matrix products, arithmetic and copies ran while one was open for 2% of the time, Pallas kernels for 0%

commit v1 on v0

v1 whole, which is shorter than its diff:
```python
import functools
import math

import jax
import jax.numpy as jnp
from jax import lax
from jax.experimental import pallas as pl
from jax.experimental.pallas import tpu as pltpu
from jax.sharding import PartitionSpec as P

MESH = pl.DeviceIdType.MESH
F32 = jnp.float32
BF16 = jnp.bfloat16
CORES = 2
CHIPS = 4
MEMBERS = CHIPS * CORES
OUT_ROWS = 6
SLOTS = 32
SCALE = 4.0 * math.log2(math.e)


class Square:
    Q, R = 8, 8

    @staticmethod
    def split(dp, sub):
        z, x, y, core = dp // 4, dp % 4, sub // 2, sub % 2
        return (z % 2) * 2 + y % 2, core, x * 2 + y // 2, z // 2

    @staticmethod
    def join(chip, core, q, r):
        z, x, y = r * 2 + chip // 2, q // 2, (q % 2) * 2 + chip % 2
        return z * 4 + x, y * 2 + core


class Line:
    Q, R = 16, 4

    @staticmethod
    def split(dp, sub):
        z, x, y, core = dp // 4, dp % 4, sub // 2, sub % 2
        return z % 4, core, x * 4 + y, z // 4

    @staticmethod
    def join(chip, core, q, r):
        return (r * 4 + chip) * 4 + q // 4, (q % 4) * 2 + core


class Column:
    Q, R = 4, 16

    @staticmethod
    def split(dp, sub):
        return sub // 2, sub % 2, dp % 4, dp // 4

    @staticmethod
    def join(chip, core, q, r):
        return r * 4 + q, chip * 2 + core


LAYOUT = Square


def iota(shape, dim):
    return lax.broadcasted_iota(jnp.int32, shape, dim)


def kernel(lay, pts_in, cand, owner, out_cent, out_mass, out_min,
           pts, pack, packs, target, dense, psum, rsend, rrecv, asend, arecv, csend, crecv,
           c_buf, cn_buf, pn_buf, acc, mass, minsend, minrecv, fsend, frecv, fsum, gsend, grecv,
           s_pack, r_pack, s_pts, r_pts, s_sib, r_sib, s_d, r_d, s_r, r_r, s_a, r_a, s_c, r_c,
           s_f, r_f, s_g, r_g, s_m, r_m):
    Q, R = lay.Q, lay.R
    per_q = R * OUT_ROWS
    rows = Q * per_q
    n_pts = pts_in.shape[0]
    rounds, per_round = cand.shape
    dp, sub = lax.axis_index("dp"), lax.axis_index("sub")
    chip, core, q_me, r_me = lay.split(dp, sub)
    member = chip * CORES + core
    device = dp * MEMBERS + sub

    def to_member(m):
        return lay.join(m // CORES, m % CORES, q_me, r_me)

    def to_plane(q):
        return lay.join(chip, core, q, r_me)

    def to_ring(r):
        return lay.join(chip, core, q_me, r)

    def copy(src, dst, send, recv, where):
        return pltpu.make_async_remote_copy(
            src_ref=src, dst_ref=dst, send_sem=send, recv_sem=recv, device_id=where, device_id_type=MESH)

    def peers(n, me):
        def wrap(body):
            def step(i, carry):
                body(lax.rem(me + i, n))
                return carry
            lax.fori_loop(1, n, step, 0)
        return wrap

    barrier = pltpu.get_barrier_semaphore()
    for n, me, to in ((MEMBERS, member, to_member), (Q, q_me, to_plane), (R, r_me, to_ring)):
        @peers(n, me)
        def _(p, to=to):
            pl.semaphore_signal(barrier, inc=1, device_id=to(p), device_id_type=MESH)

    local = iota((n_pts, 128), 0) + device * n_pts
    tiles = per_round // 128
    hit = jnp.zeros((n_pts, 128), F32)
    for rnd in range(rounds):
        for t in range(tiles):
            hit = jnp.where(local == cand[rnd:rnd + 1, 128 * t:128 * (t + 1)], 1.0, hit)
    hit = jnp.max(hit, axis=1, keepdims=True)
    below = jnp.where(iota((n_pts, n_pts), 1) < iota((n_pts, n_pts), 0), 1.0, 0.0).astype(BF16)
    rank = jnp.dot(below, jnp.broadcast_to(hit, (n_pts, 128)).astype(BF16), preferred_element_type=F32)
    lane = iota((n_pts, 128), 1)
    rank = rank.astype(jnp.int32)
    sel = jnp.where((rank == lane) & (lane < SLOTS), hit, 0.0).astype(BF16)
    picked = lax.dot_general(sel, pts_in[...], (((0,), (0,)), ((), ())), preferred_element_type=F32)
    shift = (member % 4) * SLOTS
    moved = jnp.where(rank + shift == lane, hit, 0.0)
    rowno = iota((n_pts, 128), 0)
    high = jnp.sum(moved * (rowno // 2).astype(F32), axis=0, keepdims=True)
    low = jnp.sum(moved * (rowno % 2).astype(F32), axis=0, keepdims=True)
    used = jnp.sum(moved, axis=0, keepdims=True)
    which = iota((16, 128), 0)
    ids = jnp.where(which == 0, high, jnp.where(which == 1, low, jnp.where(which == 2, used, 0.0)))
    pack[0:SLOTS, :] = picked[0:SLOTS, 0:128].astype(BF16)
    pack[SLOTS:2 * SLOTS, :] = picked[0:SLOTS, 128:256].astype(BF16)
    pack[2 * SLOTS:2 * SLOTS + 16, :] = ids.astype(BF16)
    packs[member] = pack[...]
    pts[member] = pts_in[...]

    pl.semaphore_wait(barrier, MEMBERS + Q + R - 3)

    @peers(MEMBERS, member)
    def _(p):
        copy(pack, packs.at[member], s_pack.at[p], r_pack.at[member], to_member(p)).start()

    @peers(CHIPS, chip)
    def _(p):
        copy(pts_in, pts.at[member], s_pts.at[p], r_pts.at[chip], lay.join(p, core, q_me, r_me)).start()

    sibling = lay.join(chip, 1 - core, q_me, r_me)
    copy(pts_in, pts.at[member], s_sib.at[chip], r_sib.at[chip], sibling).start()

    for blk in range(rows // 128):
        i = iota((128, 128), 0) + 128 * blk
        group = (i * 10923) // 65536
        qq, rr, jj = group // R, group % R, i - group * OUT_ROWS
        ddp, dsub = lay.join(chip, core, qq, rr)
        slot = (ddp * MEMBERS + dsub) * OUT_ROWS + jj
        found = jnp.zeros((128, 128), F32)
        for rnd in range(rounds):
            for t in range(tiles):
                c = cand[rnd:rnd + 1, 128 * t:128 * (t + 1)].astype(F32)
                o = owner[rnd * tiles + t:rnd * tiles + t + 1, :]
                found = jnp.where(slot == o, c, found)
        target[128 * blk:128 * (blk + 1), :] = jnp.broadcast_to(
            jnp.sum(found, axis=1, keepdims=True), (128, 128))

    @peers(MEMBERS, member)
    def _(p):
        copy(pack, packs.at[p], s_pack.at[p], r_pack.at[p], to_member(p)).wait_recv()

    hots = []
    for half in range(2):
        ident = jnp.zeros((1, 128), F32)
        for m in range(4 * half, 4 * half + 4):
            mdp, msub = to_member(m)
            tile = packs[m, 2 * SLOTS:2 * SLOTS + 16, :].astype(F32)
            first = ((mdp * MEMBERS + msub) * n_pts + 1).astype(F32)
            ident = ident + 2.0 * tile[0:1, :] + tile[1:2, :] + first * tile[2:3, :]
        hots.append(jnp.where(target[...] + 1.0 == ident, 1.0, 0.0).astype(BF16))
    hot = jnp.concatenate(hots, axis=1)
    left = jnp.dot(hot, packs[:, 0:SLOTS, :].reshape(MEMBERS * SLOTS, 128), preferred_element_type=F32)
    right = jnp.dot(hot, packs[:, SLOTS:2 * SLOTS, :].reshape(MEMBERS * SLOTS, 128), preferred_element_type=F32)
    for q in range(Q):
        both = jnp.concatenate([left[per_q * q:per_q * (q + 1)], right[per_q * q:per_q * (q + 1)]], axis=0)
        dense[q] = both.astype(BF16)

    @peers(Q, q_me)
    def _(p):
        copy(dense.at[p], crecv.at[q_me], s_d.at[p], r_d.at[q_me], to_plane(p)).start()

    psum[...] = dense[q_me].astype(F32)

    @peers(Q, q_me)
    def _(p):
        copy(dense.at[p], crecv.at[p], s_d.at[p], r_d.at[p], to_plane(p)).wait_recv()
        psum[...] += crecv[p].astype(F32)

    for r in range(R):
        a = psum[OUT_ROWS * r:OUT_ROWS * (r + 1), :]
        b = psum[per_q + OUT_ROWS * r:per_q + OUT_ROWS * (r + 1), :]
        pad = jnp.zeros((2, 128), F32)
        rsend[r] = jnp.concatenate([a, pad, b, pad], axis=0).astype(BF16)

    @peers(R, r_me)
    def _(p):
        copy(rsend.at[p], rrecv.at[r_me], s_r.at[p], r_r.at[r_me], to_ring(p)).start()

    gsend[0] = rsend[r_me].astype(F32)

    @peers(R, r_me)
    def _(p):
        copy(rsend.at[p], rrecv.at[p], s_r.at[p], r_r.at[p], to_ring(p)).wait_recv()
        gsend[0] += rrecv[p].astype(F32)

    asend[...] = gsend[0].astype(BF16)
    arecv[r_me] = asend[...]

    @peers(R, r_me)
    def _(p):
        copy(asend, arecv.at[r_me], s_a.at[p], r_a.at[r_me], to_ring(p)).start()

    @peers(R, r_me)
    def _(p):
        copy(asend, arecv.at[p], s_a.at[p], r_a.at[p], to_ring(p)).wait_recv()

    for r in range(R):
        tile = arecv[r].astype(F32)
        psum[OUT_ROWS * r:OUT_ROWS * (r + 1), :] = tile[0:OUT_ROWS, :]
        psum[per_q + OUT_ROWS * r:per_q + OUT_ROWS * (r + 1), :] = tile[8:8 + OUT_ROWS, :]
    csend[...] = psum[...].astype(BF16)

    @peers(Q, q_me)
    def _(p):
        copy(csend, c_buf.at[q_me], s_c.at[p], r_c.at[q_me], to_plane(p)).start()

    c_buf[q_me] = csend[...]

    @peers(CHIPS, chip)
    def _(p):
        slot = pts.at[p * CORES + core]
        copy(pts_in, slot, s_pts.at[p], r_pts.at[p], lay.join(p, core, q_me, r_me)).wait_recv()
        copy(slot, slot, s_sib.at[p], r_sib.at[p], sibling).start()

    @peers(Q, q_me)
    def _(p):
        copy(csend, c_buf.at[p], s_c.at[p], r_c.at[p], to_plane(p)).wait_recv()

    lefts = jnp.concatenate([c_buf[q, 0:per_q, :].astype(F32) for q in range(Q)], axis=0)
    rights = jnp.concatenate([c_buf[q, per_q:2 * per_q, :].astype(F32) for q in range(Q)], axis=0)
    chosen = jnp.concatenate([lefts, rights], axis=1)
    cn_buf[...] = jnp.broadcast_to(jnp.sum(chosen * chosen, axis=1, keepdims=True), (rows, 128))
    pn_buf[...] = (2.0 * chosen).astype(BF16)
    acc[...] = jnp.zeros_like(acc)
    mass[...] = jnp.zeros_like(mass)

    def block(idx):
        part = pts[idx]
        wide = part.astype(F32)
        square = wide * wide
        top = square.astype(BF16)
        rest = (square - top.astype(F32)).astype(BF16)
        ones = jnp.ones((8, part.shape[1]), BF16)
        nt = (((1,), (1,)), ((), ()))
        pn = (lax.dot_general(ones, top, nt, preferred_element_type=F32)
              + lax.dot_general(ones, rest, nt, preferred_element_type=F32))[0:1, :]
        dots = lax.dot_general(pn_buf[...], part, nt, preferred_element_type=F32)
        less = dots - cn_buf[:, 0:1]
        near = pn - jnp.max(less, axis=0, keepdims=True)
        weight = jnp.exp2((less - pn) * SCALE).astype(BF16)
        acc[...] += jnp.dot(weight, part, preferred_element_type=F32)
        wide_w = weight.astype(F32)
        m = wide_w[:, 0:128]
        for t in range(1, n_pts // 128):
            m = m + wide_w[:, 128 * t:128 * (t + 1)]
        mass[...] += m
        for t in range(n_pts // 128):
            minsend[idx, t:t + 1, :] = near[:, 128 * t:128 * (t + 1)]

    def same_core(i, carry):
        block(lax.rem(chip + i, CHIPS) * CORES + core)
        return carry

    def other_core(i, carry):
        p = lax.rem(chip + i, CHIPS)
        slot = pts.at[p * CORES + 1 - core]
        copy(slot, slot, s_sib.at[p], r_sib.at[p], sibling).wait_recv()
        block(p * CORES + 1 - core)
        return carry

    lax.fori_loop(0, CHIPS, same_core, 0)
    lax.fori_loop(0, CHIPS, other_core, 0)

    total = jnp.sum(mass[...], axis=1, keepdims=True)
    diag = iota((per_q, 128), 0) == iota((per_q, 128), 1)
    for q in range(Q):
        lo, hi = per_q * q, per_q * (q + 1)
        fsend[q, 0:per_q, :] = acc[lo:hi, 0:128]
        fsend[q, per_q:2 * per_q, :] = acc[lo:hi, 128:256]
        line = jnp.sum(jnp.where(diag, total[lo:hi], 0.0), axis=0, keepdims=True)
        fsend[q, 2 * per_q:2 * per_q + 8, :] = jnp.broadcast_to(line, (8, 128))

    @peers(Q, q_me)
    def _(p):
        copy(fsend.at[p], frecv.at[q_me], s_f.at[p], r_f.at[q_me], to_plane(p)).start()

    @peers(MEMBERS, member)
    def _(p):
        copy(minsend.at[p], minrecv.at[member], s_m.at[p], r_m.at[member], to_member(p)).start()

    fsum[...] = fsend[q_me]

    @peers(Q, q_me)
    def _(p):
        copy(fsend.at[p], frecv.at[p], s_f.at[p], r_f.at[p], to_plane(p)).wait_recv()
        fsum[...] += frecv[p]

    for r in range(R):
        lo, hi = OUT_ROWS * r, OUT_ROWS * (r + 1)
        gsend[r, 0:OUT_ROWS, :] = fsum[lo:hi, :]
        gsend[r, OUT_ROWS:8, :] = fsum[2 * per_q:2 * per_q + 8 - OUT_ROWS, :]
        gsend[r, 8:8 + OUT_ROWS, :] = fsum[per_q + lo:per_q + hi, :]
        gsend[r, 8 + OUT_ROWS:16, :] = jnp.zeros((8 - OUT_ROWS, 128), F32)

    @peers(R, r_me)
    def _(p):
        copy(gsend.at[p], grecv.at[r_me], s_g.at[p], r_g.at[r_me], to_ring(p)).start()

    out_min[...] = minsend[member]

    @peers(MEMBERS, member)
    def _(p):
        copy(minsend.at[p], minrecv.at[p], s_m.at[p], r_m.at[p], to_member(p)).wait_recv()
        out_min[...] = jnp.minimum(out_min[...], minrecv[p])

    final = fsum.at[0:16]
    final[...] = gsend[r_me]

    @peers(R, r_me)
    def _(p):
        copy(gsend.at[p], grecv.at[p], s_g.at[p], r_g.at[p], to_ring(p)).wait_recv()
        final[...] += grecv[p]

    both = final[...]
    line = both[OUT_ROWS:OUT_ROWS + 1, :]
    pick = iota((8, 128), 1) == iota((8, 128), 0) + OUT_ROWS * r_me
    column = jnp.sum(jnp.where(pick, line, 0.0), axis=1, keepdims=True)
    out_cent[:, 0:128] = both[0:OUT_ROWS, :] / column[0:OUT_ROWS]
    out_cent[:, 128:256] = both[8:8 + OUT_ROWS, :] / column[0:OUT_ROWS]
    eye = iota((8, 128), 1) == iota((8, 128), 0)
    out_mass[...] = jnp.sum(jnp.where(eye, column, 0.0), axis=0, keepdims=True)

    @peers(MEMBERS, member)
    def _(p):
        copy(pack, packs.at[member], s_pack.at[p], r_pack.at[p], to_member(p)).wait_send()
        copy(minsend.at[p], minrecv.at[p], s_m.at[p], r_m.at[p], to_member(p)).wait_send()

    @peers(CHIPS, chip)
    def _(p):
        slot = pts.at[p * CORES + core]
        copy(pts_in, slot, s_pts.at[p], r_pts.at[p], sibling).wait_send()
        copy(slot, slot, s_sib.at[p], r_sib.at[p], sibling).wait_send()

    copy(pts_in, pts.at[member], s_sib.at[chip], r_sib.at[chip], sibling).wait_send()

    @peers(Q, q_me)
    def _(p):
        copy(dense.at[p], crecv.at[p], s_d.at[p], r_d.at[p], sibling).wait_send()
        copy(csend, c_buf.at[p], s_c.at[p], r_c.at[p], sibling).wait_send()
        copy(fsend.at[p], frecv.at[p], s_f.at[p], r_f.at[p], sibling).wait_send()

    @peers(R, r_me)
    def _(p):
        copy(rsend.at[p], rrecv.at[p], s_r.at[p], r_r.at[p], sibling).wait_send()
        copy(asend, arecv.at[p], s_a.at[p], r_a.at[p], sibling).wait_send()
        copy(gsend.at[p], grecv.at[p], s_g.at[p], r_g.at[p], sibling).wait_send()


def on_device(lay, points, candidates, owner_slot):
    Q, R = lay.Q, lay.R
    n_pts, dim = points.shape
    per_q = R * OUT_ROWS
    rows = Q * per_q
    owner = owner_slot.reshape(-1, 128)
    vmem = pltpu.VMEM
    dma = pltpu.SemaphoreType.DMA
    scratch = [
        vmem((MEMBERS, n_pts, dim), BF16),
        vmem((2 * SLOTS + 16, 128), BF16),
        vmem((MEMBERS, 2 * SLOTS + 16, 128), BF16),
        vmem((rows, 128), F32),
        vmem((Q, 2 * per_q, 128), BF16),
        vmem((2 * per_q, 128), F32),
        vmem((R, 16, 128), BF16),
        vmem((R, 16, 128), BF16),
        vmem((16, 128), BF16),
        vmem((R, 16, 128), BF16),
        vmem((2 * per_q, 128), BF16),
        vmem((Q, 2 * per_q, 128), BF16),
        vmem((Q, 2 * per_q, 128), BF16),
        vmem((rows, 128), F32),
        vmem((rows, dim), BF16),
        vmem((rows, dim), F32),
        vmem((rows, 128), F32),
        vmem((MEMBERS, n_pts // 128, 128), F32),
        vmem((MEMBERS, n_pts // 128, 128), F32),
        vmem((Q, 2 * per_q + 8, 128), F32),
        vmem((Q, 2 * per_q + 8, 128), F32),
        vmem((2 * per_q + 8, 128), F32),
        vmem((R, 16, 128), F32),
        vmem((R, 16, 128), F32),
    ]
    for n in (MEMBERS, CHIPS, CHIPS, Q, R, R, Q, Q, R, MEMBERS):
        scratch += [dma((n,)), dma((n,))]
    cent, mass, near = pl.pallas_call(
        functools.partial(kernel, lay),
        out_shape=(
            jax.ShapeDtypeStruct((OUT_ROWS, dim), F32),
            jax.ShapeDtypeStruct((1, 128), F32),
            jax.ShapeDtypeStruct((n_pts // 128, 128), F32),
        ),
        in_specs=[pl.BlockSpec(memory_space=vmem)] * 3,
        out_specs=[pl.BlockSpec(memory_space=vmem)] * 3,
        scratch_shapes=scratch,
        compiler_params=pltpu.CompilerParams(
            collective_id=0, has_side_effects=True, vmem_limit_bytes=48 * 2 ** 20),
    )(points, candidates, owner)
    return cent, mass[0, 0:OUT_ROWS], near.reshape(-1)


def solution(mesh):
    return jax.shard_map(
        functools.partial(on_device, LAYOUT),
        mesh=mesh,
        in_specs=(P(("dp", "sub"), None), P(), P()),
        out_specs=(P(("dp", "sub"), None), P(("dp", "sub")), P(("dp", "sub"))),
        check_vma=False,
    )
```

time: 729 us -> 77.7 us (0.11)
  waiting for transfers between devices: 367 us -> 0 us
  blocking collectives: 289 us -> 0 us
  Pallas kernels: 0 us -> 72.2 us
  other arithmetic: 28.4 us -> 0 us
  local copies, waits for them, and re-layouts: 25.9 us -> 4.05 us
  between operations: 14.3 us -> 0.65 us
    unnamed x2 -> x0, waiting for transfers between devices: 367 us -> none
    psum x1 -> x0, blocking collectives: 187 us -> none  [pick_rows(): return lax.psum(picked, ('dp', 'sub')).astype(jnp.bfloat16)]
    unnamed x1 -> x0, blocking collectives: 101 us -> none
    pallas_call x0 -> x1, Pallas kernels: none -> 72.2 us  [on_device(): pl.pallas_call(functools.partial(kernel, lay), out_shape=(jax.ShapeDtypeS...]
    scatter x1 -> x0, other arithmetic: 17.2 us -> none  [on_device(): jnp.zeros((total_rows, width_dim), jnp.float32).at[owner_slot]]
    scatter x1 -> x0, local copies, waits for them, and re-layouts: 11.8 us -> none  [on_device(): jnp.zeros((total_rows,), jnp.float32).at[owner_slot].set(partial_mass)]
    gather x4 -> x0, local copies, waits for them, and re-layouts: 11.2 us -> none  [pick_rows(): points[local_row].astype(jnp.float32)]
  transfers between devices with their start and end apart: 1 -> 0, of which waited for: 1 -> 0; matrix products, arithmetic and copies ran while one was open for 2% -> 0% of each run, Pallas kernels for 0% -> 0%
where the time goes in v1:
time: 77.7 us; the launch traced here: 76.9 us
  Pallas kernels  72.2 us (93%)
  local copies, waits for them, and re-layouts  4.05 us (5%)
    pallas_call x1, Pallas kernels, on_device(): pl.pallas_call(functools.partial(kernel, lay), out_shape=(jax.ShapeDtypeS...  72.2 us
    unnamed x8, local copies, waits for them, and re-layouts  3.53 us

profile of v1, /device:TPU:6, one launch (start us, length us, event | category | flops | bytes accessed | tf_op | source)
XLA Modules:
  0.0 76.9 jit_solution(3652327561743610510)
XLA Ops:
  0.6 0.0 copy-start
  0.6 0.9 %copy-done = bf16[512,256]{1,0:T(8,128)(2,1)S(1)} copy-done((bf16[512,256]{1,0:T(8,128)(2,1)S(1)}, bf16[512,256]{1,0:T(8,128)(2,1)}, u32[]{:S(2)}) %copy-start) | copy-done | bytes 262168
  1.6 0.0 copy-start.1
  1.6 0.7 copy-done.1
  2.3 0.0 copy-start.2
  2.3 0.7 copy-done.2
  3.0 72.2 %shard_map.58 = (f32[6,256]{1,0:T(8,128)S(1)}, f32[1,128]{1,0:T(1,128)S(1)}, f32[4,128]{1,0:T(4,128)S(1)}) custom-call(bf16[512,256]{1,0:T(8,128)(2,1)S(1)} %copy-done, s32[4,768]{1,0:T(4,128)S(1)} %copy-done.1, s32[24,128]{1,0:T(8,128)S(1)} %bitcast.4), custom_call_target="tpu_custom_call" | custom-call | tf_op jit(solution)/shard_map/pallas_call | solution.py:412
  75.2 0.5 slice_bitcast_fusion
  75.7 0.6 copy.8
  76.3 0.6 copy.9
Async XLA Ops:
  0.6 1.0 %copy-start = (bf16[512,256]{1,0:T(8,128)(2,1)S(1)}, bf16[512,256]{1,0:T(8,128)(2,1)}, u32[]{:S(2)}) copy-start(bf16[512,256]{1,0:T(8,128)(2,1)} %pts_in.1) | copy-start | bytes 786436
  1.6 0.7 copy-start.1
  2.3 0.7 copy-start.2

commit v2 on v1

v2 whole, which is shorter than its diff:
```python
import math

import jax
import jax.numpy as jnp
from jax import lax
from jax.experimental import pallas as pl
from jax.experimental.pallas import tpu as pltpu
from jax.sharding import PartitionSpec as P

MESH = pl.DeviceIdType.MESH
F32 = jnp.float32
BF16 = jnp.bfloat16
CORES = 2
CHIPS = 4
MEMBERS = CHIPS * CORES
OUT_ROWS = 6
SLOTS = 32
SCALE = 4.0 * math.log2(math.e)


Q, R = 16, 4
X, Z = 4, 16


def iota(shape, dim):
    return lax.broadcasted_iota(jnp.int32, shape, dim)


def kernel(pts_hbm, cand_hbm, owner_hbm, out_cent, out_mass, out_min,
           pts, cand, owner, pack, packs, target, dense, drecv, psum, rsend, rrecv, csend, c_buf,
           cn_buf, c_twice, acc, mass, minsend, minrecv, fsend, frecv, fsum, gsend, grecv,
           s_in, s_pack, r_pack, s_pts, r_pts, s_sib, r_sib, s_d, r_d, s_r, r_r, s_c, r_c,
           s_f, r_f, s_g, r_g, s_m, r_m):
    per_q = R * OUT_ROWS
    per_x = Z * OUT_ROWS
    rows = Q * per_q
    n_pts = pts_hbm.shape[0]
    rounds, per_round = cand.shape
    tiles = per_round // 128
    dp, sub = lax.axis_index("dp"), lax.axis_index("sub")
    z, x, chip, core = dp // X, dp % X, sub // CORES, sub % CORES
    low, high = z % 4, z // 4
    q_me = x * 4 + low
    k_me = low * R + high
    device = dp * MEMBERS + sub
    sibling = (dp, chip * CORES + 1 - core)

    def to_member(m):
        return dp, m

    def to_chip(p):
        return dp, p * CORES + core

    def to_plane(q):
        return (high * 4 + q % 4) * X + q // 4, sub

    def to_ring(r):
        return (r * 4 + low) * X + x, sub

    def to_x(p):
        return z * X + p, sub

    def to_z(p):
        return p * X + x, sub

    def z_slot(p):
        return (p % 4) * R + p // 4

    def copy(src, dst, send, recv, where):
        return pltpu.make_async_remote_copy(
            src_ref=src, dst_ref=dst, send_sem=send, recv_sem=recv, device_id=where, device_id_type=MESH)

    def peers(n, me):
        def wrap(body):
            def step(i, carry):
                body(lax.rem(me + i, n))
                return carry
            lax.fori_loop(1, n, step, 0)
        return wrap

    def far_first(n, me):
        def wrap(body):
            def step(i, carry):
                body(lax.rem(me + n // 2 + (1 - 2 * (i % 2)) * ((i + 1) // 2), n))
                return carry
            lax.fori_loop(0, n - 1, step, 0)
        return wrap

    barrier = pltpu.get_barrier_semaphore()
    for order, n, me, to in ((far_first, Z, z, to_z), (peers, Q, q_me, to_plane), (peers, MEMBERS, sub, to_member)):
        @order(n, me)
        def _(p, to=to):
            pl.semaphore_signal(barrier, inc=1, device_id=to(p), device_id_type=MESH)

    loads = [
        pltpu.make_async_copy(cand_hbm, cand, s_in.at[0]),
        pltpu.make_async_copy(pts_hbm, pts.at[sub], s_in.at[1]),
        pltpu.make_async_copy(owner_hbm, owner, s_in.at[2]),
    ]
    for load in loads:
        load.start()
    for load in loads:
        load.wait()

    step = 64
    hits = []
    for lo in range(0, n_pts, step):
        local = iota((step, 128), 0) + (device * n_pts + lo)
        hit = jnp.zeros((step, 128), F32)
        for rnd in range(rounds):
            for t in range(tiles):
                hit = jnp.where(local == cand[rnd:rnd + 1, 128 * t:128 * (t + 1)], 1.0, hit)
        hits.append(jnp.max(hit, axis=1, keepdims=True))
    hit = jnp.concatenate(hits, axis=0)
    below = jnp.where(iota((n_pts, n_pts), 1) < iota((n_pts, n_pts), 0), 1.0, 0.0).astype(BF16)
    rank = jnp.dot(below, jnp.broadcast_to(hit, (n_pts, 128)).astype(BF16), preferred_element_type=F32)
    rank = rank.astype(jnp.int32)
    lane = iota((n_pts, 128), 1)
    sel = jnp.where((rank == lane) & (lane < SLOTS), hit, 0.0).astype(BF16)
    picked = lax.dot_general(sel, pts[sub], (((0,), (0,)), ((), ())), preferred_element_type=F32)
    moved = jnp.where(rank + (sub % 4) * SLOTS == lane, hit, 0.0)
    rowno = iota((n_pts, 128), 0)
    upper = jnp.sum(moved * (rowno >> 1).astype(F32), axis=0, keepdims=True)
    lower = jnp.sum(moved * (rowno & 1).astype(F32), axis=0, keepdims=True)
    used = jnp.sum(moved, axis=0, keepdims=True)
    which = iota((16, 128), 0)
    ids = jnp.where(which == 0, upper, jnp.where(which == 1, lower, jnp.where(which == 2, used, 0.0)))
    pack[0:SLOTS, :] = picked[0:SLOTS, 0:128].astype(BF16)
    pack[SLOTS:2 * SLOTS, :] = picked[0:SLOTS, 128:256].astype(BF16)
    pack[2 * SLOTS:2 * SLOTS + 16, :] = ids.astype(BF16)
    packs[sub] = pack[...]

    pl.semaphore_wait(barrier, MEMBERS + Q + Z - 3)

    @peers(MEMBERS, sub)
    def _(p):
        copy(pack, packs.at[sub], s_pack.at[p], r_pack.at[sub], to_member(p)).start()

    for blk in range(rows // 128):
        i = iota((128, 128), 0) + 128 * blk
        group = (i * 10923) >> 16
        q, r, j = group >> 2, group & 3, i - group * OUT_ROWS
        slot = ((((r << 2) + (q & 3)) * X + (q >> 2)) * MEMBERS + sub) * OUT_ROWS + j
        found = jnp.zeros((128, 128), F32)
        for rnd in range(rounds):
            for t in range(tiles):
                c = cand[rnd:rnd + 1, 128 * t:128 * (t + 1)].astype(F32)
                o = owner[rnd * tiles + t:rnd * tiles + t + 1, :]
                found = jnp.where(slot == o, c, found)
        target[128 * blk:128 * (blk + 1), :] = jnp.broadcast_to(
            jnp.sum(found, axis=1, keepdims=True), (128, 128))

    @peers(MEMBERS, sub)
    def _(p):
        copy(pack, packs.at[p], s_pack.at[p], r_pack.at[p], to_member(p)).wait_recv()

    hots = []
    for half in range(2):
        ident = jnp.zeros((1, 128), F32)
        for m in range(4 * half, 4 * half + 4):
            tile = packs[m, 2 * SLOTS:2 * SLOTS + 16, :].astype(F32)
            first = ((dp * MEMBERS + m) * n_pts + 1).astype(F32)
            ident = ident + 2.0 * tile[0:1, :] + tile[1:2, :] + first * tile[2:3, :]
        hots.append(jnp.where(target[...] + 1.0 == ident, 1.0, 0.0).astype(BF16))
    hot = jnp.concatenate(hots, axis=1)
    left = jnp.dot(hot, packs[:, 0:SLOTS, :].reshape(MEMBERS * SLOTS, 128), preferred_element_type=F32)
    right = jnp.dot(hot, packs[:, SLOTS:2 * SLOTS, :].reshape(MEMBERS * SLOTS, 128), preferred_element_type=F32)
    for q in range(Q):
        both = jnp.concatenate([left[per_q * q:per_q * (q + 1)], right[per_q * q:per_q * (q + 1)]], axis=0)
        dense[q] = both.astype(BF16)

    @far_first(Q, q_me)
    def _(p):
        copy(dense.at[p], drecv.at[q_me], s_d.at[p], r_d.at[q_me], to_plane(p)).start()

    @peers(CHIPS, chip)
    def _(p):
        copy(pts.at[sub], pts.at[sub], s_pts.at[p], r_pts.at[chip], to_chip(p)).start()

    copy(pts.at[sub], pts.at[sub], s_sib.at[chip], r_sib.at[chip], sibling).start()

    psum[...] = dense[q_me].astype(F32)

    @far_first(Q, q_me)
    def _(p):
        copy(dense.at[p], drecv.at[p], s_d.at[p], r_d.at[p], to_plane(p)).wait_recv()
        psum[...] += drecv[p].astype(F32)

    rsend[...] = psum[...].astype(BF16)

    @far_first(R, high)
    def _(p):
        copy(rsend, rrecv.at[high], s_r.at[p], r_r.at[high], to_ring(p)).start()

    @far_first(R, high)
    def _(p):
        copy(rsend, rrecv.at[p], s_r.at[p], r_r.at[p], to_ring(p)).wait_recv()
        psum[...] += rrecv[p].astype(F32)

    csend[...] = psum[...].astype(BF16)

    @far_first(Q, q_me)
    def _(p):
        copy(csend, c_buf.at[q_me], s_c.at[p], r_c.at[q_me], to_plane(p)).start()

    c_buf[q_me] = csend[...]

    @peers(CHIPS, chip)
    def _(p):
        slot = pts.at[p * CORES + core]
        copy(slot, slot, s_pts.at[p], r_pts.at[p], to_chip(p)).wait_recv()
        copy(slot, slot, s_sib.at[p], r_sib.at[p], sibling).start()

    @far_first(Q, q_me)
    def _(p):
        copy(csend, c_buf.at[p], s_c.at[p], r_c.at[p], to_plane(p)).wait_recv()

    lefts = jnp.concatenate([c_buf[q, 0:per_q, :].astype(F32) for q in range(Q)], axis=0)
    rights = jnp.concatenate([c_buf[q, per_q:2 * per_q, :].astype(F32) for q in range(Q)], axis=0)
    chosen = jnp.concatenate([lefts, rights], axis=1)
    cn_buf[...] = jnp.broadcast_to(jnp.sum(chosen * chosen, axis=1, keepdims=True), (rows, 128))
    c_twice[...] = (2.0 * chosen).astype(BF16)
    acc[...] = jnp.zeros_like(acc)
    mass[...] = jnp.zeros_like(mass)

    def block(idx):
        part = pts[idx]
        wide = part.astype(F32)
        square = wide * wide
        top = square.astype(BF16)
        rest = (square - top.astype(F32)).astype(BF16)
        ones = jnp.ones((8, part.shape[1]), BF16)
        nt = (((1,), (1,)), ((), ()))
        pn = (lax.dot_general(ones, top, nt, preferred_element_type=F32)
              + lax.dot_general(ones, rest, nt, preferred_element_type=F32))[0:1, :]
        dots = lax.dot_general(c_twice[...], part, nt, preferred_element_type=F32)
        less = dots - cn_buf[:, 0:1]
        near = pn - jnp.max(less, axis=0, keepdims=True)
        weight = jnp.exp2((less - pn) * SCALE).astype(BF16)
        acc[...] += jnp.dot(weight, part, preferred_element_type=F32)
        wide_w = weight.astype(F32)
        m = wide_w[:, 0:128]
        for t in range(1, n_pts // 128):
            m = m + wide_w[:, 128 * t:128 * (t + 1)]
        mass[...] += m
        for t in range(n_pts // 128):
            minsend[idx, t:t + 1, :] = near[:, 128 * t:128 * (t + 1)]

    def same_core(i, carry):
        block(lax.rem(chip + i, CHIPS) * CORES + core)
        return carry

    def other_core(i, carry):
        p = lax.rem(chip + i, CHIPS)
        slot = pts.at[p * CORES + 1 - core]
        copy(slot, slot, s_sib.at[p], r_sib.at[p], sibling).wait_recv()
        block(p * CORES + 1 - core)
        return carry

    lax.fori_loop(0, CHIPS, same_core, 0)
    lax.fori_loop(0, CHIPS, other_core, 0)

    total = jnp.sum(mass[...], axis=1, keepdims=True)
    diag = iota((per_x, 128), 0) == iota((per_x, 128), 1)
    for p in range(X):
        lo, hi = per_x * p, per_x * (p + 1)
        fsend[p, 0:per_x, :] = acc[lo:hi, 0:128]
        fsend[p, per_x:2 * per_x, :] = acc[lo:hi, 128:256]
        line = jnp.sum(jnp.where(diag, total[lo:hi], 0.0), axis=0, keepdims=True)
        fsend[p, 2 * per_x:2 * per_x + 8, :] = jnp.broadcast_to(line, (8, 128))

    @far_first(X, x)
    def _(p):
        copy(fsend.at[p], frecv.at[x], s_f.at[p], r_f.at[x], to_x(p)).start()

    @peers(MEMBERS, sub)
    def _(p):
        copy(minsend.at[p], minrecv.at[sub], s_m.at[p], r_m.at[sub], to_member(p)).start()

    fsum[...] = fsend[x]

    @far_first(X, x)
    def _(p):
        copy(fsend.at[p], frecv.at[p], s_f.at[p], r_f.at[p], to_x(p)).wait_recv()
        fsum[...] += frecv[p]

    for k in range(Z):
        lo, hi = OUT_ROWS * k, OUT_ROWS * (k + 1)
        gsend[k, 0:OUT_ROWS, :] = fsum[lo:hi, :]
        gsend[k, OUT_ROWS:8, :] = fsum[2 * per_x:2 * per_x + 8 - OUT_ROWS, :]
        gsend[k, 8:8 + OUT_ROWS, :] = fsum[per_x + lo:per_x + hi, :]
        gsend[k, 8 + OUT_ROWS:16, :] = jnp.zeros((8 - OUT_ROWS, 128), F32)

    @far_first(Z, z)
    def _(p):
        copy(gsend.at[z_slot(p)], grecv.at[z], s_g.at[p], r_g.at[z], to_z(p)).start()

    out_min[...] = minsend[sub]

    @peers(MEMBERS, sub)
    def _(p):
        copy(minsend.at[p], minrecv.at[p], s_m.at[p], r_m.at[p], to_member(p)).wait_recv()
        out_min[...] = jnp.minimum(out_min[...], minrecv[p])

    final = fsum.at[0:16]
    final[...] = gsend[k_me]

    @peers(Z, z)
    def _(p):
        copy(gsend.at[p], grecv.at[p], s_g.at[p], r_g.at[p], to_z(p)).wait_recv()
        final[...] += grecv[p]

    both = final[...]
    line = both[OUT_ROWS:OUT_ROWS + 1, :]
    pick = iota((8, 128), 1) == iota((8, 128), 0) + OUT_ROWS * k_me
    column = jnp.sum(jnp.where(pick, line, 0.0), axis=1, keepdims=True)
    out_cent[:, 0:128] = both[0:OUT_ROWS, :] / column[0:OUT_ROWS]
    out_cent[:, 128:256] = both[8:8 + OUT_ROWS, :] / column[0:OUT_ROWS]
    eye = iota((8, 128), 1) == iota((8, 128), 0)
    out_mass[...] = jnp.sum(jnp.where(eye, column, 0.0), axis=0, keepdims=True)

    @peers(MEMBERS, sub)
    def _(p):
        copy(pack, packs.at[sub], s_pack.at[p], r_pack.at[p], to_member(p)).wait_send()

    @peers(MEMBERS, sub)
    def _(p):
        copy(minsend.at[p], minrecv.at[p], s_m.at[p], r_m.at[p], to_member(p)).wait_send()

    @peers(CHIPS, chip)
    def _(p):
        slot = pts.at[p * CORES + core]
        copy(slot, slot, s_pts.at[p], r_pts.at[p], sibling).wait_send()
        copy(slot, slot, s_sib.at[p], r_sib.at[p], sibling).wait_send()

    copy(pts.at[sub], pts.at[sub], s_sib.at[chip], r_sib.at[chip], sibling).wait_send()

    @peers(Q, q_me)
    def _(p):
        copy(dense.at[p], drecv.at[p], s_d.at[p], r_d.at[p], sibling).wait_send()

    @peers(Q, q_me)
    def _(p):
        copy(csend, c_buf.at[p], s_c.at[p], r_c.at[p], sibling).wait_send()

    @peers(R, high)
    def _(p):
        copy(rsend, rrecv.at[p], s_r.at[p], r_r.at[p], sibling).wait_send()

    @peers(X, x)
    def _(p):
        copy(fsend.at[p], frecv.at[p], s_f.at[p], r_f.at[p], sibling).wait_send()

    @peers(Z, z)
    def _(p):
        copy(gsend.at[p], grecv.at[p], s_g.at[p], r_g.at[p], sibling).wait_send()


def on_device(points, candidates, owner_slot):
    n_pts, dim = points.shape
    per_q, per_x = R * OUT_ROWS, Z * OUT_ROWS
    rows = Q * per_q
    owner = owner_slot.reshape(-1, 128)
    vmem = pltpu.VMEM
    dma = pltpu.SemaphoreType.DMA
    scratch = [
        vmem((MEMBERS, n_pts, dim), BF16),
        vmem(candidates.shape, jnp.int32),
        vmem(owner.shape, jnp.int32),
        vmem((2 * SLOTS + 16, 128), BF16),
        vmem((MEMBERS, 2 * SLOTS + 16, 128), BF16),
        vmem((rows, 128), F32),
        vmem((Q, 2 * per_q, 128), BF16),
        vmem((Q, 2 * per_q, 128), BF16),
        vmem((2 * per_q, 128), F32),
        vmem((2 * per_q, 128), BF16),
        vmem((R, 2 * per_q, 128), BF16),
        vmem((2 * per_q, 128), BF16),
        vmem((Q, 2 * per_q, 128), BF16),
        vmem((rows, 128), F32),
        vmem((rows, dim), BF16),
        vmem((rows, dim), F32),
        vmem((rows, 128), F32),
        vmem((MEMBERS, n_pts // 128, 128), F32),
        vmem((MEMBERS, n_pts // 128, 128), F32),
        vmem((X, 2 * per_x + 8, 128), F32),
        vmem((X, 2 * per_x + 8, 128), F32),
        vmem((2 * per_x + 8, 128), F32),
        vmem((Z, 16, 128), F32),
        vmem((Z, 16, 128), F32),
        dma((3,)),
    ]
    for n in (MEMBERS, CHIPS, CHIPS, Q, R, Q, X, Z, MEMBERS):
        scratch += [dma((n,)), dma((n,))]
    cent, mass, near = pl.pallas_call(
        kernel,
        out_shape=(
            jax.ShapeDtypeStruct((OUT_ROWS, dim), F32),
            jax.ShapeDtypeStruct((1, 128), F32),
            jax.ShapeDtypeStruct((n_pts // 128, 128), F32),
        ),
        in_specs=[pl.BlockSpec(memory_space=pltpu.HBM)] * 3,
        out_specs=[pl.BlockSpec(memory_space=vmem)] * 3,
        scratch_shapes=scratch,
        compiler_params=pltpu.CompilerParams(
            collective_id=0, has_side_effects=True, vmem_limit_bytes=55213 * 2 ** 10),
    )(points, candidates, owner)
    return cent, mass[0, 0:OUT_ROWS], near.reshape(-1)


def solution(mesh):
    return jax.shard_map(
        on_device,
        mesh=mesh,
        in_specs=(P(("dp", "sub"), None), P(), P()),
        out_specs=(P(("dp", "sub"), None), P(("dp", "sub")), P(("dp", "sub"))),
        check_vma=False,
    )
```

time: 77.7 us -> 63.8 us (0.82)
  Pallas kernels: 72.2 us -> 60.7 us
  local copies, waits for them, and re-layouts: 4.05 us -> 1.69 us
    pallas_call x1, Pallas kernels: 72.2 us -> 60.7 us  [on_device(): pl.pallas_call(kernel, out_shape=(jax.ShapeDtypeStruct((OUT_ROWS, dim), F...]
    unnamed x8 -> x2, local copies, waits for them, and re-layouts: 3.53 us -> 1.18 us
where the time goes in v2:
time: 63.8 us; the launch traced here: 63 us
  Pallas kernels  60.7 us (95%)
  local copies, waits for them, and re-layouts  1.69 us (3%)
  between operations  0.64 us (1%)
    pallas_call x1, Pallas kernels, on_device(): pl.pallas_call(kernel, out_shape=(jax.ShapeDtypeStruct((OUT_ROWS, dim), F...  60.7 us

profile of v2, /device:TPU:6, one launch (start us, length us, event | category | flops | bytes accessed | tf_op | source)
XLA Modules:
  0.0 63.0 jit_solution(13501732361984280854)
XLA Ops:
  0.6 60.7 %shard_map.58 = (f32[6,256]{1,0:T(8,128)S(1)}, f32[1,128]{1,0:T(1,128)S(1)}, f32[4,128]{1,0:T(4,128)S(1)}) custom-call(bf16[512,256]{1,0:T(8,128)(2,1)} %pts_hbm.1, s32[4,768]{1,0:T(4,128)} %cand_hbm.1, s32[24,128]{1,0:T(8,128)} %bitcast.5), custom_call_target="tpu_custom_call" | custom-call | tf_op jit(solution)/shard_map/pallas_call | solution.py:395
  61.4 0.5 slice_bitcast_fusion
  61.9 0.6 copy.8
  62.5 0.6 copy.9

commit v3 on v2

--- a/solution.py
+++ b/solution.py
@@ -28,7 +28,7 @@
 
 def kernel(pts_hbm, cand_hbm, owner_hbm, out_cent, out_mass, out_min,
            pts, cand, owner, pack, packs, target, dense, drecv, psum, rsend, rrecv, csend, c_buf,
-           cn_buf, c_twice, acc, mass, minsend, minrecv, fsend, frecv, fsum, gsend, grecv,
+           pn_buf, minsend, minrecv, fsend, frecv, fsum, gsend, grecv,
            s_in, s_pack, r_pack, s_pts, r_pts, s_sib, r_sib, s_d, r_d, s_r, r_r, s_c, r_c,
            s_f, r_f, s_g, r_g, s_m, r_m):
     per_q = R * OUT_ROWS
@@ -199,9 +199,18 @@
 
     csend[...] = psum[...].astype(BF16)
 
-    @far_first(Q, q_me)
-    def _(p):
-        copy(csend, c_buf.at[q_me], s_c.at[p], r_c.at[q_me], to_plane(p)).start()
+    def wide_peers(b):
+        def wrap(body):
+            def step(i, carry):
+                body(lax.rem(x + b, X) * 4 + lax.rem(low + i, 4))
+                return carry
+            lax.fori_loop(0 if b else 1, 4, step, 0)
+        return wrap
+
+    for b in (2, 3, 1, 0):
+        @wide_peers(b)
+        def _(p):
+            copy(csend, c_buf.at[q_me], s_c.at[p], r_c.at[q_me], to_plane(p)).start()
 
     c_buf[q_me] = csend[...]
 
@@ -211,77 +220,85 @@
         copy(slot, slot, s_pts.at[p], r_pts.at[p], to_chip(p)).wait_recv()
         copy(slot, slot, s_sib.at[p], r_sib.at[p], sibling).start()
 
-    @far_first(Q, q_me)
-    def _(p):
-        copy(csend, c_buf.at[p], s_c.at[p], r_c.at[p], to_plane(p)).wait_recv()
-
-    lefts = jnp.concatenate([c_buf[q, 0:per_q, :].astype(F32) for q in range(Q)], axis=0)
-    rights = jnp.concatenate([c_buf[q, per_q:2 * per_q, :].astype(F32) for q in range(Q)], axis=0)
-    chosen = jnp.concatenate([lefts, rights], axis=1)
-    cn_buf[...] = jnp.broadcast_to(jnp.sum(chosen * chosen, axis=1, keepdims=True), (rows, 128))
-    c_twice[...] = (2.0 * chosen).astype(BF16)
-    acc[...] = jnp.zeros_like(acc)
-    mass[...] = jnp.zeros_like(mass)
-
-    def block(idx):
-        part = pts[idx]
-        wide = part.astype(F32)
+    nt = (((1,), (1,)), ((), ()))
+
+    def norms(idx):
+        wide = pts[idx].astype(F32)
         square = wide * wide
         top = square.astype(BF16)
         rest = (square - top.astype(F32)).astype(BF16)
-        ones = jnp.ones((8, part.shape[1]), BF16)
-        nt = (((1,), (1,)), ((), ()))
+        ones = jnp.ones((8, wide.shape[1]), BF16)
         pn = (lax.dot_general(ones, top, nt, preferred_element_type=F32)
-              + lax.dot_general(ones, rest, nt, preferred_element_type=F32))[0:1, :]
-        dots = lax.dot_general(c_twice[...], part, nt, preferred_element_type=F32)
-        less = dots - cn_buf[:, 0:1]
-        near = pn - jnp.max(less, axis=0, keepdims=True)
-        weight = jnp.exp2((less - pn) * SCALE).astype(BF16)
-        acc[...] += jnp.dot(weight, part, preferred_element_type=F32)
-        wide_w = weight.astype(F32)
-        m = wide_w[:, 0:128]
-        for t in range(1, n_pts // 128):
-            m = m + wide_w[:, 128 * t:128 * (t + 1)]
-        mass[...] += m
-        for t in range(n_pts // 128):
-            minsend[idx, t:t + 1, :] = near[:, 128 * t:128 * (t + 1)]
-
-    def same_core(i, carry):
-        block(lax.rem(chip + i, CHIPS) * CORES + core)
-        return carry
-
-    def other_core(i, carry):
+              + lax.dot_general(ones, rest, nt, preferred_element_type=F32))
+        pn_buf[idx] = pn[0:1, :]
+
+    @peers(CHIPS + 1, 0)
+    def _(i):
+        norms(lax.rem(chip + i, CHIPS) * CORES + core)
+
+    @peers(CHIPS + 1, 0)
+    def _(i):
         p = lax.rem(chip + i, CHIPS)
         slot = pts.at[p * CORES + 1 - core]
         copy(slot, slot, s_sib.at[p], r_sib.at[p], sibling).wait_recv()
-        block(p * CORES + 1 - core)
-        return carry
-
-    lax.fori_loop(0, CHIPS, same_core, 0)
-    lax.fori_loop(0, CHIPS, other_core, 0)
-
-    total = jnp.sum(mass[...], axis=1, keepdims=True)
+        norms(p * CORES + 1 - core)
+
     diag = iota((per_x, 128), 0) == iota((per_x, 128), 1)
-    for p in range(X):
-        lo, hi = per_x * p, per_x * (p + 1)
-        fsend[p, 0:per_x, :] = acc[lo:hi, 0:128]
-        fsend[p, per_x:2 * per_x, :] = acc[lo:hi, 128:256]
-        line = jnp.sum(jnp.where(diag, total[lo:hi], 0.0), axis=0, keepdims=True)
-        fsend[p, 2 * per_x:2 * per_x + 8, :] = jnp.broadcast_to(line, (8, 128))
+    highest = []
+    for pair in ((2, 1), (3, 0)):
+        lefts, rights = [], []
+        for b in pair:
+            @wide_peers(b)
+            def _(p):
+                copy(csend, c_buf.at[p], s_c.at[p], r_c.at[p], to_plane(p)).wait_recv()
+
+            for l in range(4):
+                rows_q = c_buf[lax.rem(x + b, X) * 4 + l].astype(F32)
+                lefts.append(rows_q[0:per_q])
+                rights.append(rows_q[per_q:2 * per_q])
+        chosen = jnp.concatenate([jnp.concatenate(lefts, axis=0), jnp.concatenate(rights, axis=0)], axis=1)
+        cn = jnp.sum(chosen * chosen, axis=1, keepdims=True)
+        twice = (2.0 * chosen).astype(BF16)
+        weights, peaks, mass = [], [], None
+        for m in range(MEMBERS):
+            dots = lax.dot_general(twice, pts[m], nt, preferred_element_type=F32)
+            less = dots - cn
+            peaks.append(jnp.max(less, axis=0, keepdims=True))
+            weight = jnp.exp2((less - pn_buf[m]) * SCALE).astype(BF16)
+            weights.append(weight)
+            wide_w = weight.astype(F32)
+            for t in range(n_pts // 128):
+                piece = wide_w[:, 128 * t:128 * (t + 1)]
+                mass = piece if mass is None else mass + piece
+        sums = jnp.dot(jnp.concatenate(weights, axis=1), pts[...].reshape(MEMBERS * n_pts, -1),
+                       preferred_element_type=F32)
+        highest.append(peaks)
+        total = jnp.sum(mass, axis=1, keepdims=True)
+        for k, b in enumerate(pair):
+            dest = fsend.at[b]
+            lo, hi = per_x * k, per_x * (k + 1)
+            dest[0:per_x, :] = sums[lo:hi, 0:128]
+            dest[per_x:2 * per_x, :] = sums[lo:hi, 128:256]
+            line = jnp.sum(jnp.where(diag, total[lo:hi], 0.0), axis=0, keepdims=True)
+            dest[2 * per_x:2 * per_x + 8, :] = jnp.broadcast_to(line, (8, 128))
+            if b:
+                p = lax.rem(x + b, X)
+                copy(dest, frecv.at[x], s_f.at[p], r_f.at[x], to_x(p)).start()
+
+    for m in range(MEMBERS):
+        near = pn_buf[m] - jnp.maximum(highest[0][m], highest[1][m])
+        for t in range(n_pts // 128):
+            minsend[m, t:t + 1, :] = near[:, 128 * t:128 * (t + 1)]
+
+    @peers(MEMBERS, sub)
+    def _(p):
+        copy(minsend.at[p], minrecv.at[sub], s_m.at[p], r_m.at[sub], to_member(p)).start()
+
+    fsum[...] = fsend[0]
 
     @far_first(X, x)
     def _(p):
-        copy(fsend.at[p], frecv.at[x], s_f.at[p], r_f.at[x], to_x(p)).start()
-
-    @peers(MEMBERS, sub)
-    def _(p):
-        copy(minsend.at[p], minrecv.at[sub], s_m.at[p], r_m.at[sub], to_member(p)).start()
-
-    fsum[...] = fsend[x]
-
-    @far_first(X, x)
-    def _(p):
-        copy(fsend.at[p], frecv.at[p], s_f.at[p], r_f.at[p], to_x(p)).wait_recv()
+        copy(frecv.at[p], frecv.at[p], s_f.at[p], r_f.at[p], to_x(p)).wait_recv()
         fsum[...] += frecv[p]
 
     for k in range(Z):
@@ -349,7 +366,7 @@
 
     @peers(X, x)
     def _(p):
-        copy(fsend.at[p], frecv.at[p], s_f.at[p], r_f.at[p], sibling).wait_send()
+        copy(frecv.at[p], frecv.at[p], s_f.at[p], r_f.at[p], sibling).wait_send()
 
     @peers(Z, z)
     def _(p):
@@ -377,10 +394,7 @@
         vmem((R, 2 * per_q, 128), BF16),
         vmem((2 * per_q, 128), BF16),
         vmem((Q, 2 * per_q, 128), BF16),
-        vmem((rows, 128), F32),
-        vmem((rows, dim), BF16),
-        vmem((rows, dim), F32),
-        vmem((rows, 128), F32),
+        vmem((MEMBERS, 1, n_pts), F32),
         vmem((MEMBERS, n_pts // 128, 128), F32),
         vmem((MEMBERS, n_pts // 128, 128), F32),
         vmem((X, 2 * per_x + 8, 128), F32),

time: 63.8 us -> 59.9 us (0.939)
  Pallas kernels: 60.7 us -> 56.6 us
    pallas_call x1, Pallas kernels: 60.7 us -> 56.6 us  [on_device(): pl.pallas_call(kernel, out_shape=(jax.ShapeDtypeStruct((OUT_ROWS, dim), F...]
where the time goes in v3:
time: 59.9 us; the launch traced here: 58.9 us
  Pallas kernels  56.6 us (94%)
  local copies, waits for them, and re-layouts  1.69 us (3%)
  between operations  0.64 us (1%)
    pallas_call x1, Pallas kernels, on_device(): pl.pallas_call(kernel, out_shape=(jax.ShapeDtypeStruct((OUT_ROWS, dim), F...  56.6 us

profile of v3, /device:TPU:6, one launch (start us, length us, event | category | flops | bytes accessed | tf_op | source)
XLA Modules:
  0.0 58.9 jit_solution(16904481763840995422)
XLA Ops:
  0.6 56.6 %shard_map.58 = (f32[6,256]{1,0:T(8,128)S(1)}, f32[1,128]{1,0:T(1,128)S(1)}, f32[4,128]{1,0:T(4,128)S(1)}) custom-call(bf16[512,256]{1,0:T(8,128)(2,1)} %pts_hbm.1, s32[4,768]{1,0:T(4,128)} %cand_hbm.1, s32[24,128]{1,0:T(8,128)} %bitcast.5), custom_call_target="tpu_custom_call" | custom-call | tf_op jit(solution)/shard_map/pallas_call | solution.py:409
  57.2 0.5 slice_bitcast_fusion
  57.7 0.6 %copy.8 = f32[6,256]{1,0:T(8,128)} copy(f32[6,256]{1,0:T(8,128)S(1)} %get-tuple-element.12) | data formatting | bytes 12288
  58.3 0.6 copy.9

commit v4 on v3

--- a/solution.py
+++ b/solution.py
@@ -20,6 +20,7 @@
 
 Q, R = 16, 4
 X, Z = 4, 16
+PACKED = 2 * OUT_ROWS + 1
 
 
 def iota(shape, dim):
@@ -41,7 +42,6 @@
     z, x, chip, core = dp // X, dp % X, sub // CORES, sub % CORES
     low, high = z % 4, z // 4
     q_me = x * 4 + low
-    k_me = low * R + high
     device = dp * MEMBERS + sub
     sibling = (dp, chip * CORES + 1 - core)
 
@@ -62,9 +62,6 @@
 
     def to_z(p):
         return p * X + x, sub
-
-    def z_slot(p):
-        return (p % 4) * R + p // 4
 
     def copy(src, dst, send, recv, where):
         return pltpu.make_async_remote_copy(
@@ -243,7 +240,7 @@
         copy(slot, slot, s_sib.at[p], r_sib.at[p], sibling).wait_recv()
         norms(p * CORES + 1 - core)
 
-    diag = iota((per_x, 128), 0) == iota((per_x, 128), 1)
+    diag = iota((per_q, 128), 0) == iota((per_q, 128), 1)
     highest = []
     for pair in ((2, 1), (3, 0)):
         lefts, rights = [], []
@@ -274,16 +271,36 @@
                        preferred_element_type=F32)
         highest.append(peaks)
         total = jnp.sum(mass, axis=1, keepdims=True)
-        for k, b in enumerate(pair):
-            dest = fsend.at[b]
-            lo, hi = per_x * k, per_x * (k + 1)
-            dest[0:per_x, :] = sums[lo:hi, 0:128]
-            dest[per_x:2 * per_x, :] = sums[lo:hi, 128:256]
-            line = jnp.sum(jnp.where(diag, total[lo:hi], 0.0), axis=0, keepdims=True)
-            dest[2 * per_x:2 * per_x + 8, :] = jnp.broadcast_to(line, (8, 128))
-            if b:
-                p = lax.rem(x + b, X)
-                copy(dest, frecv.at[x], s_f.at[p], r_f.at[x], to_x(p)).start()
+        for l in range(4):
+            for k, b in enumerate(pair):
+                dest = fsend.at[b, l]
+                lo = per_x * k + per_q * l
+                dest[0:per_q, :] = sums[lo:lo + per_q, 0:128]
+                dest[per_q:2 * per_q, :] = sums[lo:lo + per_q, 128:256]
+                line = jnp.sum(jnp.where(diag, total[lo:lo + per_q], 0.0), axis=0, keepdims=True)
+                dest[2 * per_q:2 * per_q + 8, :] = jnp.broadcast_to(line, (8, 128))
+                if b:
+                    p = lax.rem(x + b, X)
+                    copy(dest, frecv.at[x, l], s_f.at[p, l], r_f.at[x, l], to_x(p)).start()
+
+    for l in range(4):
+        part = fsend[0, l]
+        for b in (1, 2, 3):
+            p = lax.rem(x + b, X)
+            piece = frecv.at[p, l]
+            copy(piece, piece, s_f.at[p, l], r_f.at[p, l], sibling).wait_recv()
+            part = part + piece[...]
+        fsum[l] = part
+        for r in range(R):
+            p = r * 4 + l
+            lo = OUT_ROWS * r
+            gsend[p, 0:OUT_ROWS, :] = fsum[l, lo:lo + OUT_ROWS, :]
+            gsend[p, OUT_ROWS:OUT_ROWS + 1, :] = fsum[l, 2 * per_q:2 * per_q + 1, :]
+            gsend[p, OUT_ROWS + 1:PACKED, :] = fsum[l, per_q + lo:per_q + lo + OUT_ROWS, :]
+
+            @pl.when(p != z)
+            def _():
+                copy(gsend.at[p, 0:PACKED], grecv.at[z, 0:PACKED], s_g.at[p], r_g.at[z], to_z(p)).start()
 
     for m in range(MEMBERS):
         near = pn_buf[m] - jnp.maximum(highest[0][m], highest[1][m])
@@ -294,55 +311,9 @@
     def _(p):
         copy(minsend.at[p], minrecv.at[sub], s_m.at[p], r_m.at[sub], to_member(p)).start()
 
-    fsum[...] = fsend[0]
-
-    @far_first(X, x)
-    def _(p):
-        copy(frecv.at[p], frecv.at[p], s_f.at[p], r_f.at[p], to_x(p)).wait_recv()
-        fsum[...] += frecv[p]
-
-    for k in range(Z):
-        lo, hi = OUT_ROWS * k, OUT_ROWS * (k + 1)
-        gsend[k, 0:OUT_ROWS, :] = fsum[lo:hi, :]
-        gsend[k, OUT_ROWS:8, :] = fsum[2 * per_x:2 * per_x + 8 - OUT_ROWS, :]
-        gsend[k, 8:8 + OUT_ROWS, :] = fsum[per_x + lo:per_x + hi, :]
-        gsend[k, 8 + OUT_ROWS:16, :] = jnp.zeros((8 - OUT_ROWS, 128), F32)
-
-    @far_first(Z, z)
-    def _(p):
-        copy(gsend.at[z_slot(p)], grecv.at[z], s_g.at[p], r_g.at[z], to_z(p)).start()
-
-    out_min[...] = minsend[sub]
-
-    @peers(MEMBERS, sub)
-    def _(p):
-        copy(minsend.at[p], minrecv.at[p], s_m.at[p], r_m.at[p], to_member(p)).wait_recv()
-        out_min[...] = jnp.minimum(out_min[...], minrecv[p])
-
-    final = fsum.at[0:16]
-    final[...] = gsend[k_me]
-
-    @peers(Z, z)
-    def _(p):
-        copy(gsend.at[p], grecv.at[p], s_g.at[p], r_g.at[p], to_z(p)).wait_recv()
-        final[...] += grecv[p]
-
-    both = final[...]
-    line = both[OUT_ROWS:OUT_ROWS + 1, :]
-    pick = iota((8, 128), 1) == iota((8, 128), 0) + OUT_ROWS * k_me
-    column = jnp.sum(jnp.where(pick, line, 0.0), axis=1, keepdims=True)
-    out_cent[:, 0:128] = both[0:OUT_ROWS, :] / column[0:OUT_ROWS]
-    out_cent[:, 128:256] = both[8:8 + OUT_ROWS, :] / column[0:OUT_ROWS]
-    eye = iota((8, 128), 1) == iota((8, 128), 0)
-    out_mass[...] = jnp.sum(jnp.where(eye, column, 0.0), axis=0, keepdims=True)
-
     @peers(MEMBERS, sub)
     def _(p):
         copy(pack, packs.at[sub], s_pack.at[p], r_pack.at[p], to_member(p)).wait_send()
-
-    @peers(MEMBERS, sub)
-    def _(p):
-        copy(minsend.at[p], minrecv.at[p], s_m.at[p], r_m.at[p], to_member(p)).wait_send()
 
     @peers(CHIPS, chip)
     def _(p):
@@ -366,11 +337,43 @@
 
     @peers(X, x)
     def _(p):
-        copy(frecv.at[p], frecv.at[p], s_f.at[p], r_f.at[p], sibling).wait_send()
+        for l in range(4):
+            piece = frecv.at[p, l]
+            copy(piece, piece, s_f.at[p, l], r_f.at[p, l], sibling).wait_send()
+
+    out_min[...] = minsend[sub]
+
+    @peers(MEMBERS, sub)
+    def _(p):
+        copy(minsend.at[p], minrecv.at[p], s_m.at[p], r_m.at[p], to_member(p)).wait_recv()
+        out_min[...] = jnp.minimum(out_min[...], minrecv[p])
+
+    @peers(MEMBERS, sub)
+    def _(p):
+        copy(minsend.at[p], minrecv.at[p], s_m.at[p], r_m.at[p], to_member(p)).wait_send()
+
+    final = fsum.at[0, 0:16]
+    final[0:PACKED, :] = gsend[z, 0:PACKED, :]
 
     @peers(Z, z)
     def _(p):
-        copy(gsend.at[p], grecv.at[p], s_g.at[p], r_g.at[p], sibling).wait_send()
+        piece = grecv.at[p, 0:PACKED]
+        copy(piece, piece, s_g.at[p], r_g.at[p], to_z(p)).wait_send()
+
+    @peers(Z, z)
+    def _(p):
+        piece = grecv.at[p, 0:PACKED]
+        copy(piece, piece, s_g.at[p], r_g.at[p], to_z(p)).wait_recv()
+        final[0:PACKED, :] += piece[...]
+
+    both = final[...]
+    line = both[OUT_ROWS:OUT_ROWS + 1, :]
+    pick = iota((8, 128), 1) == iota((8, 128), 0) + OUT_ROWS * high
+    column = jnp.sum(jnp.where(pick, line, 0.0), axis=1, keepdims=True)
+    out_cent[:, 0:128] = both[0:OUT_ROWS, :] / column[0:OUT_ROWS]
+    out_cent[:, 128:256] = both[OUT_ROWS + 1:PACKED, :] / column[0:OUT_ROWS]
+    eye = iota((8, 128), 1) == iota((8, 128), 0)
+    out_mass[...] = jnp.sum(jnp.where(eye, column, 0.0), axis=0, keepdims=True)
 
 
 def on_device(points, candidates, owner_slot):
@@ -397,15 +400,15 @@
         vmem((MEMBERS, 1, n_pts), F32),
         vmem((MEMBERS, n_pts // 128, 128), F32),
         vmem((MEMBERS, n_pts // 128, 128), F32),
-        vmem((X, 2 * per_x + 8, 128), F32),
-        vmem((X, 2 * per_x + 8, 128), F32),
-        vmem((2 * per_x + 8, 128), F32),
+        vmem((X, 4, 2 * per_q + 8, 128), F32),
+        vmem((X, 4, 2 * per_q + 8, 128), F32),
+        vmem((4, 2 * per_q + 8, 128), F32),
         vmem((Z, 16, 128), F32),
         vmem((Z, 16, 128), F32),
         dma((3,)),
     ]
-    for n in (MEMBERS, CHIPS, CHIPS, Q, R, Q, X, Z, MEMBERS):
-        scratch += [dma((n,)), dma((n,))]
+    for n in ((MEMBERS,), (CHIPS,), (CHIPS,), (Q,), (R,), (Q,), (X, 4), (Z,), (MEMBERS,)):
+        scratch += [dma(n), dma(n)]
     cent, mass, near = pl.pallas_call(
         kernel,
         out_shape=(

time: 59.9 us -> 58.6 us (0.978); the launches traced: 58.9 us -> 58.4 us
  no operation moved by 1% of the time
where the time goes in v4:
time: 58.6 us; the launch traced here: 58.4 us
  Pallas kernels  56.1 us (96%)
  local copies, waits for them, and re-layouts  1.69 us (3%)
  between operations  0.64 us (1%)
    pallas_call x1, Pallas kernels, on_device(): pl.pallas_call(kernel, out_shape=(jax.ShapeDtypeStruct((OUT_ROWS, dim), F...  56.1 us
    unnamed x2, local copies, waits for them, and re-layouts  1.18 us

profile of v4, /device:TPU:6, one launch (start us, length us, event | category | flops | bytes accessed | tf_op | source)
XLA Modules:
  0.0 58.4 jit_solution(15576029016364785004)
XLA Ops:
  0.6 56.1 %shard_map.58 = (f32[6,256]{1,0:T(8,128)S(1)}, f32[1,128]{1,0:T(1,128)S(1)}, f32[4,128]{1,0:T(4,128)S(1)}) custom-call(bf16[512,256]{1,0:T(8,128)(2,1)} %pts_hbm.1, s32[4,768]{1,0:T(4,128)} %cand_hbm.1, s32[24,128]{1,0:T(8,128)} %bitcast.5), custom_call_target="tpu_custom_call" | custom-call | tf_op jit(solution)/shard_map/pallas_call | solution.py:412
  56.7 0.5 slice_bitcast_fusion
  57.2 0.6 %copy.8 = f32[6,256]{1,0:T(8,128)} copy(f32[6,256]{1,0:T(8,128)S(1)} %get-tuple-element.12) | data formatting | bytes 12288
  57.8 0.6 copy.9

commit v5 on v4

--- a/solution.py
+++ b/solution.py
@@ -27,7 +27,7 @@
     return lax.broadcasted_iota(jnp.int32, shape, dim)
 
 
-def kernel(pts_hbm, cand_hbm, owner_hbm, out_cent, out_mass, out_min,
+def kernel(pts_hbm, cand_hbm, owner_hbm, out_sums, out_min,
            pts, cand, owner, pack, packs, target, dense, drecv, psum, rsend, rrecv, csend, c_buf,
            pn_buf, minsend, minrecv, fsend, frecv, fsum, gsend, grecv,
            s_in, s_pack, r_pack, s_pts, r_pts, s_sib, r_sib, s_d, r_d, s_r, r_r, s_c, r_c,
@@ -366,14 +366,19 @@
         copy(piece, piece, s_g.at[p], r_g.at[p], to_z(p)).wait_recv()
         final[0:PACKED, :] += piece[...]
 
-    both = final[...]
-    line = both[OUT_ROWS:OUT_ROWS + 1, :]
+    out_sums[...] = final[...]
+
+
+def finish(sums, near, out_cent, out_mass, out_min):
+    high = lax.axis_index("dp") // X // 4
+    line = sums[OUT_ROWS:OUT_ROWS + 1, :]
     pick = iota((8, 128), 1) == iota((8, 128), 0) + OUT_ROWS * high
     column = jnp.sum(jnp.where(pick, line, 0.0), axis=1, keepdims=True)
-    out_cent[:, 0:128] = both[0:OUT_ROWS, :] / column[0:OUT_ROWS]
-    out_cent[:, 128:256] = both[OUT_ROWS + 1:PACKED, :] / column[0:OUT_ROWS]
+    out_cent[:, 0:128] = sums[0:OUT_ROWS, :] / column[0:OUT_ROWS]
+    out_cent[:, 128:256] = sums[OUT_ROWS + 1:PACKED, :] / column[0:OUT_ROWS]
     eye = iota((8, 128), 1) == iota((8, 128), 0)
-    out_mass[...] = jnp.sum(jnp.where(eye, column, 0.0), axis=0, keepdims=True)
+    out_mass[...] = jnp.sum(jnp.where(eye, column, 0.0), axis=0, keepdims=True)[:, 0:OUT_ROWS]
+    out_min[...] = near[...]
 
 
 def on_device(points, candidates, owner_slot):
@@ -409,20 +414,30 @@
     ]
     for n in ((MEMBERS,), (CHIPS,), (CHIPS,), (Q,), (R,), (Q,), (X, 4), (Z,), (MEMBERS,)):
         scratch += [dma(n), dma(n)]
-    cent, mass, near = pl.pallas_call(
+    sums, near = pl.pallas_call(
         kernel,
         out_shape=(
-            jax.ShapeDtypeStruct((OUT_ROWS, dim), F32),
-            jax.ShapeDtypeStruct((1, 128), F32),
+            jax.ShapeDtypeStruct((16, 128), F32),
             jax.ShapeDtypeStruct((n_pts // 128, 128), F32),
         ),
         in_specs=[pl.BlockSpec(memory_space=pltpu.HBM)] * 3,
-        out_specs=[pl.BlockSpec(memory_space=vmem)] * 3,
+        out_specs=[pl.BlockSpec(memory_space=vmem)] * 2,
         scratch_shapes=scratch,
         compiler_params=pltpu.CompilerParams(
             collective_id=0, has_side_effects=True, vmem_limit_bytes=55213 * 2 ** 10),
     )(points, candidates, owner)
-    return cent, mass[0, 0:OUT_ROWS], near.reshape(-1)
+    cent, mass, near = pl.pallas_call(
+        finish,
+        out_shape=(
+            jax.ShapeDtypeStruct((OUT_ROWS, dim), F32),
+            jax.ShapeDtypeStruct((1, OUT_ROWS), F32),
+            jax.ShapeDtypeStruct((n_pts // 128, 128), F32),
+        ),
+        in_specs=[pl.BlockSpec(memory_space=vmem)] * 2,
+        out_specs=[pl.BlockSpec(memory_space=vmem)] * 3,
+        compiler_params=pltpu.CompilerParams(vmem_limit_bytes=2 ** 20),
+    )(sums, near)
+    return cent, mass.reshape(-1), near.reshape(-1)
 
 
 def solution(mesh):

time: 58.6 us -> 57.6 us (0.983)
  local copies, waits for them, and re-layouts: 1.69 us -> 0 us
  Pallas kernels: 56.1 us -> 56.8 us
    unnamed x2 -> x0, local copies, waits for them, and re-layouts: 1.18 us -> none
    pallas_call x1 -> x2, Pallas kernels: 56.1 us -> 56.8 us  [the longest x1 56.1 us: on_device(): pl.pallas_call(kernel, out_shape=(jax.ShapeDtypeStruct((16, 128), F32), j...]
where the time goes in v5:
time: 57.6 us; the launch traced here: 57.4 us
  Pallas kernels  56.8 us (99%)
  between operations  0.64 us (1%)
    pallas_call x1, Pallas kernels, on_device(): pl.pallas_call(kernel, out_shape=(jax.ShapeDtypeStruct((16, 128), F32), j...  56.1 us

profile of v5, /device:TPU:6, one launch (start us, length us, event | category | flops | bytes accessed | tf_op | source)
XLA Modules:
  0.0 57.4 jit_solution(11533618349457467937)
XLA Ops:
  0.6 56.1 %shard_map.58 = (f32[16,128]{1,0:T(8,128)S(1)}, f32[4,128]{1,0:T(4,128)S(1)}) custom-call(bf16[512,256]{1,0:T(8,128)(2,1)} %pts_hbm.1, s32[4,768]{1,0:T(4,128)} %cand_hbm.1, s32[24,128]{1,0:T(8,128)} %bitcast.3), custom_call_target="tpu_custom_call" | custom-call | tf_op jit(solution)/shard_map/pallas_call | solution.py:417
  56.7 0.7 %shard_map.59 = (f32[6,256]{1,0:T(8,128)}, f32[1,6]{1,0:T(1,128)}, f32[4,128]{1,0:T(4,128)}) custom-call(f32[16,128]{1,0:T(8,128)S(1)} %get-tuple-element.8.sums, f32[4,128]{1,0:T(4,128)S(1)} %get-tuple-element.9.near), custom_call_target="tpu_custom_call" | custom-call | tf_op jit(solution)/shard_map/pallas_call | solution.py:429

commit v6 on v5

--- a/solution.py
+++ b/solution.py
@@ -20,6 +20,7 @@
 
 Q, R = 16, 4
 X, Z = 4, 16
+PIECE = 2 * R * OUT_ROWS + 1
 PACKED = 2 * OUT_ROWS + 1
 
 
@@ -83,12 +84,6 @@
             lax.fori_loop(0, n - 1, step, 0)
         return wrap
 
-    barrier = pltpu.get_barrier_semaphore()
-    for order, n, me, to in ((far_first, Z, z, to_z), (peers, Q, q_me, to_plane), (peers, MEMBERS, sub, to_member)):
-        @order(n, me)
-        def _(p, to=to):
-            pl.semaphore_signal(barrier, inc=1, device_id=to(p), device_id_type=MESH)
-
     loads = [
         pltpu.make_async_copy(cand_hbm, cand, s_in.at[0]),
         pltpu.make_async_copy(pts_hbm, pts.at[sub], s_in.at[1]),
@@ -96,8 +91,14 @@
     ]
     for load in loads:
         load.start()
-    for load in loads:
-        load.wait()
+
+    barrier = pltpu.get_barrier_semaphore()
+    for order, n, me, to in ((far_first, Z, z, to_z), (peers, Q, q_me, to_plane), (peers, MEMBERS, sub, to_member)):
+        @order(n, me)
+        def _(p, to=to):
+            pl.semaphore_signal(barrier, inc=1, device_id=to(p), device_id_type=MESH)
+
+    loads[0].wait()
 
     step = 64
     hits = []
@@ -114,6 +115,7 @@
     rank = rank.astype(jnp.int32)
     lane = iota((n_pts, 128), 1)
     sel = jnp.where((rank == lane) & (lane < SLOTS), hit, 0.0).astype(BF16)
+    loads[1].wait()
     picked = lax.dot_general(sel, pts[sub], (((0,), (0,)), ((), ())), preferred_element_type=F32)
     moved = jnp.where(rank + (sub % 4) * SLOTS == lane, hit, 0.0)
     rowno = iota((n_pts, 128), 0)
@@ -129,9 +131,11 @@
 
     pl.semaphore_wait(barrier, MEMBERS + Q + Z - 3)
 
-    @peers(MEMBERS, sub)
+    @far_first(MEMBERS, sub)
     def _(p):
         copy(pack, packs.at[sub], s_pack.at[p], r_pack.at[sub], to_member(p)).start()
+
+    loads[2].wait()
 
     for blk in range(rows // 128):
         i = iota((128, 128), 0) + 128 * blk
@@ -278,19 +282,19 @@
                 dest[0:per_q, :] = sums[lo:lo + per_q, 0:128]
                 dest[per_q:2 * per_q, :] = sums[lo:lo + per_q, 128:256]
                 line = jnp.sum(jnp.where(diag, total[lo:lo + per_q], 0.0), axis=0, keepdims=True)
-                dest[2 * per_q:2 * per_q + 8, :] = jnp.broadcast_to(line, (8, 128))
+                dest[2 * per_q:PIECE, :] = line
                 if b:
                     p = lax.rem(x + b, X)
-                    copy(dest, frecv.at[x, l], s_f.at[p, l], r_f.at[x, l], to_x(p)).start()
+                    copy(dest.at[0:PIECE], frecv.at[x, l, 0:PIECE], s_f.at[p, l], r_f.at[x, l], to_x(p)).start()
 
     for l in range(4):
-        part = fsend[0, l]
+        part = fsend[0, l, 0:PIECE]
         for b in (1, 2, 3):
             p = lax.rem(x + b, X)
-            piece = frecv.at[p, l]
+            piece = frecv.at[p, l, 0:PIECE]
             copy(piece, piece, s_f.at[p, l], r_f.at[p, l], sibling).wait_recv()
             part = part + piece[...]
-        fsum[l] = part
+        fsum[l, 0:PIECE, :] = part
         for r in range(R):
             p = r * 4 + l
             lo = OUT_ROWS * r
@@ -338,7 +342,7 @@
     @peers(X, x)
     def _(p):
         for l in range(4):
-            piece = frecv.at[p, l]
+            piece = frecv.at[p, l, 0:PIECE]
             copy(piece, piece, s_f.at[p, l], r_f.at[p, l], sibling).wait_send()
 
     out_min[...] = minsend[sub]

time: 57.6 us -> 56.3 us (0.977)
  Pallas kernels: 56.8 us -> 55.5 us
    pallas_call x1, Pallas kernels: 56.1 us -> 54.8 us  [on_device(): pl.pallas_call(kernel, out_shape=(jax.ShapeDtypeStruct((16, 128), F32), j...]
where the time goes in v6:
time: 56.3 us; the launch traced here: 56.1 us
  Pallas kernels  55.5 us (99%)
  between operations  0.64 us (1%)
    pallas_call x1, Pallas kernels, on_device(): pl.pallas_call(kernel, out_shape=(jax.ShapeDtypeStruct((16, 128), F32), j...  54.8 us

profile of v6, /device:TPU:6, one launch (start us, length us, event | category | flops | bytes accessed | tf_op | source)
XLA Modules:
  0.0 56.1 jit_solution(3204070595134395244)
XLA Ops:
  0.6 54.8 %shard_map.58 = (f32[16,128]{1,0:T(8,128)S(1)}, f32[4,128]{1,0:T(4,128)S(1)}) custom-call(bf16[512,256]{1,0:T(8,128)(2,1)} %pts_hbm.1, s32[4,768]{1,0:T(4,128)} %cand_hbm.1, s32[24,128]{1,0:T(8,128)} %bitcast.3), custom_call_target="tpu_custom_call" | custom-call | tf_op jit(solution)/shard_map/pallas_call | solution.py:421
  55.4 0.7 %shard_map.59 = (f32[6,256]{1,0:T(8,128)}, f32[1,6]{1,0:T(1,128)}, f32[4,128]{1,0:T(4,128)}) custom-call(f32[16,128]{1,0:T(8,128)S(1)} %get-tuple-element.8.sums, f32[4,128]{1,0:T(4,128)S(1)} %get-tuple-element.9.near), custom_call_target="tpu_custom_call" | custom-call | tf_op jit(solution)/shard_map/pallas_call | solution.py:433

commit v7 on v6

--- a/solution.py
+++ b/solution.py
@@ -227,7 +227,8 @@
         wide = pts[idx].astype(F32)
         square = wide * wide
         top = square.astype(BF16)
-        rest = (square - top.astype(F32)).astype(BF16)
+        wide_top = top.astype(F32)
+        rest = jnp.where(wide_top == square, 0.0, square - wide_top).astype(BF16)
         ones = jnp.ones((8, wide.shape[1]), BF16)
         pn = (lax.dot_general(ones, top, nt, preferred_element_type=F32)
               + lax.dot_general(ones, rest, nt, preferred_element_type=F32))
@@ -246,9 +247,9 @@
 
     diag = iota((per_q, 128), 0) == iota((per_q, 128), 1)
     highest = []
-    for pair in ((2, 1), (3, 0)):
+    for group in ((2, 1), (3,), (0,)):
         lefts, rights = [], []
-        for b in pair:
+        for b in group:
             @wide_peers(b)
             def _(p):
                 copy(csend, c_buf.at[p], s_c.at[p], r_c.at[p], to_plane(p)).wait_recv()
@@ -276,7 +277,7 @@
         highest.append(peaks)
         total = jnp.sum(mass, axis=1, keepdims=True)
         for l in range(4):
-            for k, b in enumerate(pair):
+            for k, b in enumerate(group):
                 dest = fsend.at[b, l]
                 lo = per_x * k + per_q * l
                 dest[0:per_q, :] = sums[lo:lo + per_q, 0:128]
@@ -307,11 +308,14 @@
                 copy(gsend.at[p, 0:PACKED], grecv.at[z, 0:PACKED], s_g.at[p], r_g.at[z], to_z(p)).start()
 
     for m in range(MEMBERS):
-        near = pn_buf[m] - jnp.maximum(highest[0][m], highest[1][m])
+        peak = highest[0][m]
+        for other in highest[1:]:
+            peak = jnp.maximum(peak, other[m])
+        near = pn_buf[m] - peak
         for t in range(n_pts // 128):
             minsend[m, t:t + 1, :] = near[:, 128 * t:128 * (t + 1)]
 
-    @peers(MEMBERS, sub)
+    @far_first(MEMBERS, sub)
     def _(p):
         copy(minsend.at[p], minrecv.at[sub], s_m.at[p], r_m.at[sub], to_member(p)).start()
 

time: 56.3 us -> 56.1 us (level)
  no operation moved by 1% of the time
where the time goes in v7:
time: 56.1 us; the launch traced here: 55.9 us
  Pallas kernels  55.3 us (99%)
  between operations  0.64 us (1%)
    pallas_call x1, Pallas kernels, on_device(): pl.pallas_call(kernel, out_shape=(jax.ShapeDtypeStruct((16, 128), F32), j...  54.6 us

profile of v7, /device:TPU:6, one launch (start us, length us, event | category | flops | bytes accessed | tf_op | source)
XLA Modules:
  0.0 55.9 jit_solution(1902138704070700990)
XLA Ops:
  0.6 54.6 %shard_map.58 = (f32[16,128]{1,0:T(8,128)S(1)}, f32[4,128]{1,0:T(4,128)S(1)}) custom-call(bf16[512,256]{1,0:T(8,128)(2,1)} %pts_hbm.1, s32[4,768]{1,0:T(4,128)} %cand_hbm.1, s32[24,128]{1,0:T(8,128)} %bitcast.3), custom_call_target="tpu_custom_call" | custom-call | tf_op jit(solution)/shard_map/pallas_call | solution.py:425
  55.2 0.7 %shard_map.59 = (f32[6,256]{1,0:T(8,128)}, f32[1,6]{1,0:T(1,128)}, f32[4,128]{1,0:T(4,128)}) custom-call(f32[16,128]{1,0:T(8,128)S(1)} %get-tuple-element.8.sums, f32[4,128]{1,0:T(4,128)S(1)} %get-tuple-element.9.near), custom_call_target="tpu_custom_call" | custom-call | tf_op jit(solution)/shard_map/pallas_call | solution.py:437
